TPU v7x, 32 devices: a whole 2x2x4 slice. The times are simulated.
32 devices in a mesh: runs: 2 (over x), gx: 16 (over z, y, core).
Axes of the slice: x: 2, y: 2, z: 4, core: 2. Of those that a mesh axis runs over, the one named last changes fastest.
Arguments:
- frac: float32 [3, 524288], P(None, ('runs', 'gx')), parts along dimension 1, may hold values from 0 to 1
- velocity: float32 [3, 524288], P(None, ('runs', 'gx')), parts along dimension 1, may hold values from -6 to 6
- mass: float32 [524288], P(('runs', 'gx')), parts along dimension 0, may hold values from 0.5 to 2
- particle_cell: int32 [524288], P(('runs', 'gx')), parts along dimension 0, may hold values from 0 to 8191, as said below
- tile_count: int32 [32], P(('runs', 'gx')), parts along dimension 0, may hold values from 2048 to 16384, as said below
- time_step: float32 [2], P('runs'), parts along dimension 0, may hold values from 0.1 to 0.2
Outputs:
- new_frac: float32 [3, 524288], P(None, ('runs', 'gx')), parts along dimension 1
- new_velocity: float32 [3, 524288], P(None, ('runs', 'gx')), parts along dimension 1
- next_step: float32 [2], P('runs'), parts along dimension 0
There are 2 independent parts, one for each index of `runs`. A program takes and returns all parts, laid end to end along the dimension named above; each array names one. Nothing has to cross between parts.
Inputs may be any that keep to these rules, and one draw needn't show every extreme that they name: `particle_cell`: within each tile the slots' cell numbers never fall; live slots come first and lie in cells with z <= 126; empty slots name the tile's last cell. `tile_count`: some tile is full in every run.
All inputs are finite; a program needn't handle non-finite values.
Results may differ from a plain program's by a relative error of at most 0.0003.
Values sent between devices are 32-bit elements; how exact they have to be, the bound alone decides.
No kernel may reach another device: no remote copies, remote signals or barrier semaphores. Data moves between devices by JAX's collectives and lax.ppermute only.
A program may use at most 64 MiB of HBM per device.

v0:
```python
import functools

import jax
import jax.numpy as jnp
from jax import lax
from jax.experimental import pallas as pl
from jax.experimental.pallas import tpu as pltpu
from jax.sharding import PartitionSpec as P

CX = 2
NY = 32
NZ = 128
ROWS = CX * NY
BLOCK = 256
LANES = 128
UNROLL = 8
SPREAD = 32
TABLE = 16

mass_floor = 0.25
stiffness = 2.0
press_floor = 1.0
grain_size = 0.5
inertia_ref = 0.3
mu_static = 0.38
mu_limit = 0.64
rate_floor = 0.5
gravity = (0.5, 0.0, -0.866)
flip_share = 0.95
courant = 0.4
wave_speed = 2.0
components = ((0, 3, 4), (3, 1, 5), (4, 5, 2))
f32 = jnp.float32
bf16 = jnp.bfloat16


def split_pair(values):
    high = values.astype(bf16)
    low = (values - high.astype(f32)).astype(bf16)
    return high, low


def one_hot(cells_ref, block, offset):
    rel = cells_ref[pl.ds(block * 2, 2), :] - offset
    nodes = lax.broadcasted_iota(jnp.int32, (NZ, LANES), 0)
    halves = [jnp.where(nodes == rel[h : h + 1, :], 1.0, 0.0) for h in range(2)]
    return jnp.concatenate(halves, axis=1).astype(bf16)


def list_visits(cells_ref, count, plan_ref):
    blocks = cells_ref.shape[0] // 2
    shape = (blocks, LANES)
    number = lax.broadcasted_iota(jnp.int32, shape, 0)
    lane = lax.broadcasted_iota(jnp.int32, shape, 1)
    first_half = cells_ref[pl.ds(0, blocks, stride=2), :]
    second_half = cells_ref[pl.ds(1, blocks, stride=2), :]
    slot = number * BLOCK + lane
    reached = jnp.maximum(
        jnp.where(slot < count, first_half, 0), jnp.where(slot + LANES < count, second_half, 0)
    )
    live = number * BLOCK < count
    first = jnp.min(first_half, axis=1, keepdims=True) >> 7
    last = jnp.max(reached, axis=1, keepdims=True) >> 7
    low = jnp.where(live, first + number, 2 * LANES)
    high = jnp.where(live, last + number, -1)
    inside = (low <= lane) & (lane <= high)
    place = lane[:1]
    block = jnp.max(jnp.where(inside, number, -1), axis=0, keepdims=True)
    valid = block >= 0
    row = place - block
    plan_ref[0:1, :] = jnp.where(valid, block, 0)
    plan_ref[1:2, :] = jnp.where(valid, row + (row >> 5), 0)
    plan_ref[2:3, :] = jnp.where(valid, row, ROWS) * NZ
    plan_ref[3:4, :] = jnp.max(high, axis=0, keepdims=True) + 1
    plan_ref[4:5, :] = jnp.broadcast_to(count, (1, LANES))
    plan_ref[5:8, :] = jnp.zeros((3, LANES), jnp.int32)


def spread_kernel(
    count_ref, frac_hbm, vel_hbm, mass_hbm, cells_hbm,
    far_ref, near_ref, plan_ref, frac_ref, vel_ref, cells_ref,
    listed_ref, mass_ref, q_ref, acc_ref, sems,
):
    slots = frac_ref.shape[1]
    sources = (cells_hbm, frac_hbm, vel_hbm, mass_hbm)
    targets = (cells_ref, frac_ref, vel_ref, mass_ref)
    arrivals = [
        pltpu.make_async_copy(source, target, sems.at[k])
        for k, (source, target) in enumerate(zip(sources, targets))
    ]
    for arrival in arrivals:
        arrival.start()
    acc_ref[...] = jnp.zeros_like(acc_ref)
    arrivals[0].wait()
    count = count_ref[0]
    list_visits(cells_ref, count, plan_ref)
    listing = pltpu.make_async_copy(plan_ref, listed_ref, sems.at[4])
    listing.start()
    for arrival in arrivals[1:]:
        arrival.wait()
    sublane = lax.broadcasted_iota(jnp.int32, (8, LANES), 0)
    lane = lax.broadcasted_iota(jnp.int32, (1, LANES), 1)
    top_z = sublane >= 4
    field = sublane & 3

    def weigh(part):
        at = pl.multiple_of(part * LANES, LANES)
        here = pl.ds(at, LANES)

        def spread_out(line):
            return jnp.broadcast_to(line, (8, LANES))

        fx, fy, fz = (spread_out(frac_ref[d : d + 1, here]) for d in range(3))
        vx, vy, vz = (spread_out(vel_ref[d : d + 1, here]) for d in range(3))
        held = spread_out(jnp.where(at + lane < count, mass_ref[pl.ds(part, 1), :], 0.0))
        carried = jnp.where(
            field == 0, held, held * jnp.where(field == 1, vx, jnp.where(field == 2, vy, vz))
        )
        carried = carried * jnp.where(top_z, fz, 1.0 - fz)
        lower, upper = carried * (1.0 - fx), carried * fx
        rows = jnp.concatenate(
            [lower * (1.0 - fy), lower * fy, upper * (1.0 - fy), upper * fy], axis=0
        )
        high, low = split_pair(rows)
        q_ref[pl.ds(part, 1)] = jnp.concatenate([high, low], axis=0)[None]

    def prepare(group, carry):
        for u in range(UNROLL):
            weigh(group * UNROLL + u)
        return carry

    lax.fori_loop(0, slots // LANES // UNROLL, prepare, 0)
    listing.wait()
    total = listed_ref[3, 0]

    def visit(group, carry):
        found = []
        for u in range(UNROLL):
            v = group * UNROLL + u
            block = listed_ref[0, v]
            hot = one_hot(cells_ref, block, listed_ref[2, v])
            both = q_ref[pl.ds(block * 2, 2)]
            both = lax.dot_general(
                jnp.concatenate([both[0], both[1]], axis=1),
                hot,
                (((1,), (1,)), ((), ())),
                preferred_element_type=f32,
            )
            found.append((listed_ref[1, v], both[:SPREAD] + both[SPREAD:]))
        for base, part in found:
            for k, ahead in enumerate((0, 1, NY + 1, NY + 2)):
                at = pl.ds(pl.multiple_of((base + ahead) * 8, 8), 8)
                acc_ref[at, :] += part[8 * k : 8 * k + 8]
        return carry

    lax.fori_loop(0, (total + UNROLL - 1) // UNROLL, visit, 0)

    layers = []
    for l in range(CX + 1):
        first = l * (NY + 1) * 8
        acc_ref[first : first + 8, :] += acc_ref[first + NY * 8 : first + NY * 8 + 8, :]
        for f in range(4):
            lower = acc_ref[pl.ds(first + f, NY, stride=8), :]
            upper = acc_ref[pl.ds(first + 4 + f, NY, stride=8), :]
            layers.append(lower + pltpu.roll(upper, 1, 1))
    odd = lax.axis_index("gx") % 2 == 1
    for l in range(CX):
        for f in range(4):
            low, high = layers[l * 4 + f], layers[(l + 1) * 4 + f]
            near_ref[f * CX + l] = jnp.where(odd, low, high)
            far_ref[f * CX + l] = jnp.where(odd, high, low)


def pair_up(field, axis):
    return field + pltpu.roll(field, field.shape[axis] - 1, axis)


def step_up(field, axis):
    return pltpu.roll(field, field.shape[axis] - 1, axis) - field


def pair_down(field, axis):
    return field + pltpu.roll(field, 1, axis)


def step_down(field, axis):
    return field - pltpu.roll(field, 1, axis)


def cell_stress(vel_lo, vel_hi, mass_lo, mass_hi, keep):
    grads = []
    for a in range(3):
        diff = vel_hi[a] - vel_lo[a]
        both = vel_hi[a] + vel_lo[a]
        grads.append(
            [
                0.25 * pair_up(pair_up(diff, 0), 1),
                0.25 * pair_up(step_up(both, 0), 1),
                0.25 * step_up(pair_up(both, 0), 1),
            ]
        )
    density = 0.125 * pair_up(pair_up(mass_hi + mass_lo, 0), 1)
    dxx = grads[0][0]
    dyy = grads[1][1]
    dzz = grads[2][2]
    dxy = 0.5 * (grads[0][1] + grads[1][0])
    dxz = 0.5 * (grads[0][2] + grads[2][0])
    dyz = 0.5 * (grads[1][2] + grads[2][1])
    second = dxx * dxx + dyy * dyy + dzz * dzz + 2.0 * (dxy * dxy + dxz * dxz + dyz * dyz)
    rate = jnp.sqrt(2.0 * second + rate_floor * rate_floor)
    pressure = stiffness * density
    inertial = rate * grain_size / jnp.sqrt(pressure + press_floor)
    friction = mu_static + (mu_limit - mu_static) * inertial / (inertia_ref + inertial)
    twice = 2.0 * friction * pressure / rate
    sigma = [
        twice * dxx - pressure,
        twice * dyy - pressure,
        twice * dzz - pressure,
        twice * dxy,
        twice * dxz,
        twice * dyz,
    ]
    return [jnp.where(keep, s, 0.0) for s in sigma]


def node_force(lower, upper):
    force = []
    for a in range(3):
        sx, sy, sz = (components[a][b] for b in range(3))
        along = pair_down(pair_down(upper[sx] - lower[sx], 0), 1)
        across = step_down(pair_down(upper[sy] + lower[sy], 1), 0)
        upward = step_down(pair_down(upper[sz] + lower[sz], 0), 1)
        force.append(0.25 * (along + across + upward))
    return force


def collect_kernel(
    step_ref, plan_ref, near_ref, far_ref, far_new_ref, near_new_ref, frac_ref, vel_ref, cells_ref,
    out_ref, top_ref, listed_ref, tab_ref, pair_ref, sem,
):
    blocks = frac_ref.shape[1] // BLOCK
    listing = pltpu.make_async_copy(plan_ref, listed_ref, sem)
    listing.start()
    step = step_ref[0]
    odd = lax.axis_index("gx") % 2 == 1

    def pick(if_odd, if_even):
        return [jnp.where(odd, if_odd[k], if_even[k]) for k in range(4 * CX)]

    low, high = pick(near_ref, far_ref), pick(far_ref, near_ref)
    left, right = pick(near_new_ref, far_new_ref), pick(far_new_ref, near_new_ref)
    nodes = [
        [left[f * 2] for f in range(4)],
        [low[f * 2] + left[f * 2 + 1] for f in range(4)],
        [low[f * 2 + 1] for f in range(4)],
        [high[f * 2 + 1] + right[f * 2] for f in range(4)],
        [right[f * 2 + 1] for f in range(4)],
    ]
    height = lax.broadcasted_iota(jnp.int32, (NY, NZ), 1)
    keep = height < NZ - 1
    above_bed = height > 0
    floor = [jnp.maximum(layer[0], mass_floor) for layer in nodes]
    v_old = [[layer[1 + a] / floor[l] for a in range(3)] for l, layer in enumerate(nodes)]
    sigma = [
        cell_stress(v_old[l], v_old[l + 1], nodes[l][0], nodes[l + 1][0], keep) for l in range(4)
    ]
    blank = jnp.zeros((NY, NZ), f32)
    for l in range(CX + 1):
        force = node_force(sigma[l], sigma[l + 1])
        fields = [blank] * 8
        for a in range(3):
            layer = nodes[l + 1]
            fresh = (layer[1 + a] + step * (force[a] + layer[0] * gravity[a])) / floor[l + 1]
            fresh = jnp.where(above_bed, fresh, 0.0)
            fields[a] = fresh - flip_share * v_old[l + 1][a]
            fields[4 + a] = step * fresh
        for k, value in enumerate(fields):
            start = l * NY * TABLE + k
            tab_ref[pl.ds(start, NY, stride=TABLE), :] = value
            tab_ref[pl.ds(start + 8, NY, stride=TABLE), :] = pltpu.roll(value, NZ - 1, 1)

    for l in range(CX + 1):

        def split_row(j, carry):
            at = pl.ds(pl.multiple_of((l * NY + j) * TABLE, TABLE), TABLE)
            high, low = split_pair(tab_ref[at, :])
            pair_ref[pl.ds(l * (NY + 1) + j, 1)] = jnp.concatenate([high, low], axis=0)[None]
            return carry

        lax.fori_loop(0, NY, split_row, 0, unroll=8)
        pair_ref[l * (NY + 1) + NY] = pair_ref[l * (NY + 1)]

    out_ref[...] = jnp.zeros_like(out_ref)
    listing.wait()
    total = listed_ref[3, 0]
    count = listed_ref[4, 0]

    def visit(group, carry):
        found = []
        for u in range(UNROLL):
            v = group * UNROLL + u
            block = listed_ref[0, v]
            base = listed_ref[1, v]
            hot = one_hot(cells_ref, block, listed_ref[2, v])
            rows = [pair_ref[base + ahead] for ahead in (0, 1, NY + 1, NY + 2)]
            both = jnp.dot(jnp.concatenate(rows, axis=0), hot, preferred_element_type=f32)
            corners = []
            for k in range(4):
                four = both[4 * 8 * k : 4 * 8 * (k + 1)]
                corners += [four[0:8] + four[16:24], four[8:16] + four[24:32]]
            frac = frac_ref[:, pl.ds(pl.multiple_of(block * BLOCK, BLOCK), BLOCK)]
            for d in (2, 1, 0):
                share = frac[d : d + 1, :]
                corners = [
                    corners[k] + share * (corners[k + 1] - corners[k])
                    for k in range(0, len(corners), 2)
                ]
            found.append((block, corners[0]))
        for block, part in found:
            out_ref[pl.ds(block, 1)] += part[None]
        return carry

    lax.fori_loop(0, (total + UNROLL - 1) // UNROLL, visit, 0)

    lane = lax.broadcasted_iota(jnp.int32, (1, BLOCK), 1)

    def finish(block, top):
        at = pl.multiple_of(block * BLOCK, BLOCK)
        alive = at + lane < count
        got = out_ref[pl.ds(block, 1)][0]
        fresh = jnp.where(alive, flip_share * vel_ref[:, pl.ds(at, BLOCK)] + got[0:3], 0.0)
        out_ref[pl.ds(block, 1), 0:3] = fresh[None]
        square = fresh[0:1] * fresh[0:1] + fresh[1:2] * fresh[1:2] + fresh[2:3] * fresh[2:3]
        return jnp.maximum(top, square)

    top = lax.fori_loop(0, blocks, finish, jnp.zeros((1, BLOCK), f32), unroll=4)
    top = jnp.sqrt(jnp.max(top, axis=1, keepdims=True))
    top_ref[...] = jnp.broadcast_to(top, top_ref.shape)


def finish_kernel(plan_ref, moved_ref, frac_ref, new_frac_ref, new_vel_ref):
    blocks = frac_ref.shape[1] // BLOCK
    count = plan_ref[4:5, :]
    count = jnp.concatenate([count, count], axis=1)
    lane = lax.broadcasted_iota(jnp.int32, (1, BLOCK), 1)

    def finish(block, carry):
        at = pl.multiple_of(block * BLOCK, BLOCK)
        got = moved_ref[pl.ds(block, 1)][0]
        new_vel_ref[:, pl.ds(at, BLOCK)] = got[0:3]
        placed = jnp.where(at + lane < count, frac_ref[:, pl.ds(at, BLOCK)] + got[4:7], 0.0)
        new_frac_ref[:, pl.ds(at, BLOCK)] = placed
        return carry

    lax.fori_loop(0, blocks, finish, 0, unroll=4)


def largest(value, axis):
    devices = lax.axis_size(axis)
    value = jnp.maximum(value, lax.ppermute(value, axis, [(i, i ^ 1) for i in range(devices)]))
    odd = range(1, devices, 2)
    reach = 2
    while reach < devices:
        if devices & (devices - 1) == 0:
            pairs = [(i, i ^ reach) for i in odd]
        else:
            pairs = [(i, (i + reach) % devices) for i in odd]
        value = jnp.maximum(value, lax.ppermute(value, axis, pairs))
        reach *= 2
    return jnp.maximum(value, lax.ppermute(value, axis, [(i, i - 1) for i in odd]))


smem = pl.BlockSpec(memory_space=pltpu.SMEM)
vmem = pl.BlockSpec(memory_space=pltpu.VMEM)
hbm = pl.BlockSpec(memory_space=pltpu.HBM)


def body(frac, velocity, mass, particle_cell, tile_count, time_step):
    slots = frac.shape[1]
    blocks = slots // BLOCK
    rows = slots // LANES
    inputs = (frac, velocity, mass.reshape(rows, LANES), particle_cell.reshape(rows, LANES))
    layer_pair = pltpu.VMEM((4 * CX, NY, NZ), f32)
    far, near, plan, frac_here, vel_here, cells_here = pl.pallas_call(
        spread_kernel,
        out_shape=(
            layer_pair,
            layer_pair,
            pltpu.VMEM((8, LANES), jnp.int32),
            pltpu.VMEM(frac.shape, f32),
            pltpu.VMEM(velocity.shape, f32),
            pltpu.VMEM((rows, LANES), jnp.int32),
        ),
        in_specs=[smem] + [hbm] * 4,
        out_specs=(vmem,) * 6,
        scratch_shapes=[
            pltpu.SMEM((8, LANES), jnp.int32),
            pltpu.VMEM((rows, LANES), f32),
            pltpu.VMEM((rows, 2 * SPREAD, LANES), bf16),
            pltpu.VMEM(((CX + 1) * (NY + 1) * 8, NZ), f32),
            pltpu.SemaphoreType.DMA((5,)),
        ],
        compiler_params=pltpu.CompilerParams(vmem_limit_bytes=32 * 1024 * 1024),
        name="spread",
    )(tile_count, *[pltpu.with_memory_space_constraint(x, pltpu.HBM) for x in inputs])
    devices = lax.axis_size("gx")
    far_pairs = [(i, (i + (1 if i % 2 else -1)) % devices) for i in range(devices)]
    near_pairs = [(i, i ^ 1) for i in range(devices)]
    near_new = lax.ppermute(near, "gx", near_pairs)
    far_new = lax.ppermute(far, "gx", far_pairs)
    moved, top = pl.pallas_call(
        collect_kernel,
        out_shape=(
            jax.ShapeDtypeStruct((blocks, 8, BLOCK), f32),
            jax.ShapeDtypeStruct((8, LANES), f32),
        ),
        in_specs=[smem] + [vmem] * 8,
        out_specs=(vmem, vmem),
        scratch_shapes=[
            pltpu.SMEM((8, LANES), jnp.int32),
            pltpu.VMEM(((CX + 1) * NY * TABLE, NZ), f32),
            pltpu.VMEM(((CX + 1) * (NY + 1), 2 * TABLE, NZ), bf16),
            pltpu.SemaphoreType.DMA,
        ],
        compiler_params=pltpu.CompilerParams(vmem_limit_bytes=32 * 1024 * 1024),
        name="collect",
    )(time_step, plan, near, far, far_new, near_new, frac_here, vel_here, cells_here)
    new_frac, new_velocity = pl.pallas_call(
        finish_kernel,
        out_shape=(
            jax.ShapeDtypeStruct(frac.shape, f32),
            jax.ShapeDtypeStruct(velocity.shape, f32),
        ),
        in_specs=[vmem] * 3,
        out_specs=(vmem, vmem),
        compiler_params=pltpu.CompilerParams(vmem_limit_bytes=32 * 1024 * 1024),
        cost_estimate=pl.CostEstimate(flops=0, bytes_accessed=8000000, transcendentals=0),
        name="finish",
    )(plan, moved, frac_here)
    fastest = largest(top, "gx")
    next_step = (courant / (fastest + wave_speed))[0, :1]
    return (new_frac, new_velocity, next_step)


def solution(mesh):
    placed = (
        P(None, ("runs", "gx")),
        P(None, ("runs", "gx")),
        P(("runs", "gx")),
        P(("runs", "gx")),
        P(("runs", "gx")),
        P("runs"),
    )
    return jax.shard_map(
        body,
        mesh=mesh,
        in_specs=placed,
        out_specs=(P(None, ("runs", "gx")), P(None, ("runs", "gx")), P("runs")),
        check_vma=False,
    )
```

profile of v0, /device:TPU:0, one launch (start us, length us, event | category | flops | bytes accessed | tf_op | source)
XLA Modules:
  0.0 40.9 jit_solution(13853934077674598802)
XLA Ops:
  1.3 6.1 %spread.1 = (f32[8,32,128]{2,1,0:T(8,128)S(1)}, f32[8,32,128]{2,1,0:T(8,128)S(1)}, s32[8,128]{1,0:T(8,128)S(1)}, f32[3,16384]{1,0:T(4,128)S(1)}, f32[3,16384]{1,0:T(4,128)S(1)}, /*index=5*/s32[128,128]{1,0:T(8,128)S(1)}) custom-call(s32[1]{0:T(128)S(6)} %copy.9.count_ref, f32[3,16384]{1,0:T(4,128)} %frac_hbm.1, f32[3,16384]{1,0:T(4,128)} %vel_hbm.1, ...), custom_call_target="tpu_custom_call" | custom-call | tf_op jit(solution)/shard_map/spread/pallas_call | solution.py:384
  7.4 1.1 %collective-permute-start.1 = (f32[8,32,128]{2,1,0:T(8,128)S(1)}, f32[8,32,128]{2,1,0:T(8,128)S(1)}, u32[]{:S(2)}, u32[]{:S(2)}) collective-permute-start(f32[8,32,128]{2,1,0:T(8,128)S(1)} %get-tuple-element.14.near_ref), channel_id=1, source_target_pairs={{0,1},{1,0},{2,3},{3,2},{4,5},{5,4},{6,7},{7,6},{8,9},{9,8},{10,11... | collective-permute-start | bytes 393224 | tf_op jit(solution)/shard_map/ppermute | solution.py:409
  8.6 6.0 %collective-permute-start = (f32[8,32,128]{2,1,0:T(8,128)S(1)}, f32[8,32,128]{2,1,0:T(8,128)S(1)}, u32[]{:S(2)}, u32[]{:S(2)}) collective-permute-start(f32[8,32,128]{2,1,0:T(8,128)S(1)} %get-tuple-element.15.far_ref), channel_id=1, source_target_pairs={{0,15},{1,2},{2,1},{3,4},{4,3},{5,6},{6,5},{7,8},{8,7},{9,10},{10,... | collective-permute-start | bytes 393224 | tf_op jit(solution)/shard_map/ppermute | solution.py:410
  15.2 0.0 collective-permute-done.1.near_new_ref
  15.2 2.0 %collective-permute-done.far_new_ref = f32[8,32,128]{2,1,0:T(8,128)S(1)} collective-permute-done((f32[8,32,128]{2,1,0:T(8,128)S(1)}, f32[8,32,128]{2,1,0:T(8,128)S(1)}, u32[]{:S(2)}, u32[]{:S(2)}) %collective-permute-start) | collective-permute-done | bytes 131104 | tf_op jit(solution)/shard_map/ppermute | solution.py:410
  17.2 5.9 %collect.1 = (f32[64,8,256]{2,1,0:T(8,128)S(1)}, f32[8,128]{1,0:T(8,128)S(1)}) custom-call(f32[1]{0:T(128)S(6)} %copy.10.step_ref, s32[8,128]{1,0:T(8,128)S(1)} %get-tuple-element.13.plan_ref, f32[8,32,128]{2,1,0:T(8,128)S(1)} %get-tuple-element.14.near_ref, f32[8,32,128]{2,1,0:T(8,128)S(1)} %get-tuple-element.15.far_ref, ...), custom_call_target="tpu_custom_call" | custom-call | tf_op jit(solution)/shard_map/collect/pallas_call | solution.py:411
  23.1 0.1 collective-permute-start.2
  23.2 1.2 %collective-permute-done.2 = f32[8,128]{1,0:T(8,128)S(1)} collective-permute-done((f32[8,128]{1,0:T(8,128)S(1)}, f32[8,128]{1,0:T(8,128)S(1)}, u32[]{:S(2)}, u32[]{:S(2)}) %collective-permute-start.2) | collective-permute-done | bytes 4128 | tf_op jit(solution)/shard_map/ppermute | solution.py:360
  24.4 0.7 %collective-permute-start.3 = (f32[8,128]{1,0:T(8,128)S(1)}, f32[8,128]{1,0:T(8,128)S(1)}, u32[]{:S(2)}, u32[]{:S(2)}) collective-permute-start(f32[8,128]{1,0:T(8,128)S(1)} %max.15), channel_id=1, source_target_pairs={{1,3},{3,1},{5,7},{7,5},{9,11},{11,9},{13,15},{15,13},{17,19},{19,... | collective-permute-start | bytes 12296 | tf_op jit(solution)/shard_map/ppermute | solution.py:368
  25.0 0.0 collective-permute-done.3
  25.0 0.7 %collective-permute-start.4 = (f32[8,128]{1,0:T(8,128)S(1)}, f32[8,128]{1,0:T(8,128)S(1)}, u32[]{:S(2)}, u32[]{:S(2)}) collective-permute-start(f32[8,128]{1,0:T(8,128)S(1)} %max.16), channel_id=1, source_target_pairs={{1,5},{3,7},{5,1},{7,3},{9,13},{11,15},{13,9},{15,11},{17,21},{19,... | collective-permute-start | bytes 12296 | tf_op jit(solution)/shard_map/ppermute | solution.py:368
  25.7 0.0 collective-permute-done.4
  25.7 0.7 %collective-permute-start.5 = (f32[8,128]{1,0:T(8,128)S(1)}, f32[8,128]{1,0:T(8,128)S(1)}, u32[]{:S(2)}, u32[]{:S(2)}) collective-permute-start(f32[8,128]{1,0:T(8,128)S(1)} %max.17), channel_id=1, source_target_pairs={{1,9},{3,11},{5,13},{7,15},{9,1},{11,3},{13,5},{15,7},{17,25},{19,... | collective-permute-start | bytes 12296 | tf_op jit(solution)/shard_map/ppermute | solution.py:368
  26.4 0.0 collective-permute-done.5
  26.4 1.3 %collective-permute-start.6 = (f32[8,128]{1,0:T(8,128)S(1)}, f32[8,128]{1,0:T(8,128)S(1)}, u32[]{:S(2)}, u32[]{:S(2)}) collective-permute-start(f32[8,128]{1,0:T(8,128)S(1)} %max.18), channel_id=1, source_target_pairs={{1,0},{3,2},{5,4},{7,6},{9,8},{11,10},{13,12},{15,14},{17,16},{19,... | collective-permute-start | bytes 12296 | tf_op jit(solution)/shard_map/ppermute | solution.py:370
  27.7 1.0 %finish.1 = (f32[3,16384]{1,0:T(4,128)}, f32[3,16384]{1,0:T(4,128)}) custom-call(s32[8,128]{1,0:T(8,128)S(1)} %get-tuple-element.13.plan_ref, f32[64,8,256]{2,1,0:T(8,128)S(1)} %get-tuple-element.19.moved_ref, f32[3,16384]{1,0:T(4,128)S(1)} %get-tuple-element.16.frac_ref), custom_call_target="tpu_custom_call" | custom-call | bytes 8000000 | tf_op jit(solution)/shard_map/finish/pallas_call | solution.py:428
  28.7 11.6 %collective-permute-done.6 = f32[8,128]{1,0:T(8,128)S(1)} collective-permute-done((f32[8,128]{1,0:T(8,128)S(1)}, f32[8,128]{1,0:T(8,128)S(1)}, u32[]{:S(2)}, u32[]{:S(2)}) %collective-permute-start.6) | collective-permute-done | bytes 4128 | tf_op jit(solution)/shard_map/ppermute | solution.py:370
  40.4 0.5 %slice.3 = f32[1,1]{1,0:T(1,128)} slice(f32[8,128]{1,0:T(8,128)S(1)} %add_divide_fusion), slice={[0:1], [0:1]} | slice | bytes 8 | tf_op jit(solution)/shard_map/slice | solution.py:441
  (5 shorter events, 0.0 us)
Async XLA Ops:
  7.4 7.8 %collective-permute-start.1 = (f32[8,32,128]{2,1,0:T(8,128)S(1)}, f32[8,32,128]{2,1,0:T(8,128)S(1)}, u32[]{:S(2)}, u32[]{:S(2)}) collective-permute-start(f32[8,32,128]{2,1,0:T(8,128)S(1)} %get-tuple-element.14.near_ref), channel_id=1, source_target_pairs={{0,1},{1,0},{2,3},{3,2},{4,5},{5,4},{6,7},{7,6},{8,9},{9,8},{10,11... | collective-permute-start | bytes 393224 | tf_op jit(solution)/shard_map/ppermute | solution.py:409
  8.6 8.6 %collective-permute-start = (f32[8,32,128]{2,1,0:T(8,128)S(1)}, f32[8,32,128]{2,1,0:T(8,128)S(1)}, u32[]{:S(2)}, u32[]{:S(2)}) collective-permute-start(f32[8,32,128]{2,1,0:T(8,128)S(1)} %get-tuple-element.15.far_ref), channel_id=1, source_target_pairs={{0,15},{1,2},{2,1},{3,4},{4,3},{5,6},{6,5},{7,8},{8,7},{9,10},{10,... | collective-permute-start | bytes 393224 | tf_op jit(solution)/shard_map/ppermute | solution.py:410
  23.1 1.2 %collective-permute-start.2 = (f32[8,128]{1,0:T(8,128)S(1)}, f32[8,128]{1,0:T(8,128)S(1)}, u32[]{:S(2)}, u32[]{:S(2)}) collective-permute-start(f32[8,128]{1,0:T(8,128)S(1)} %get-tuple-element.22), channel_id=1, source_target_pairs={{0,1},{1,0},{2,3},{3,2},{4,5},{5,4},{6,7},{7,6},{8,9},{9,8},{10,11... | collective-permute-start | bytes 12296 | tf_op jit(solution)/shard_map/ppermute | solution.py:360
  24.4 0.7 %collective-permute-start.3 = (f32[8,128]{1,0:T(8,128)S(1)}, f32[8,128]{1,0:T(8,128)S(1)}, u32[]{:S(2)}, u32[]{:S(2)}) collective-permute-start(f32[8,128]{1,0:T(8,128)S(1)} %max.15), channel_id=1, source_target_pairs={{1,3},{3,1},{5,7},{7,5},{9,11},{11,9},{13,15},{15,13},{17,19},{19,... | collective-permute-start | bytes 12296 | tf_op jit(solution)/shard_map/ppermute | solution.py:368
  25.0 0.7 %collective-permute-start.4 = (f32[8,128]{1,0:T(8,128)S(1)}, f32[8,128]{1,0:T(8,128)S(1)}, u32[]{:S(2)}, u32[]{:S(2)}) collective-permute-start(f32[8,128]{1,0:T(8,128)S(1)} %max.16), channel_id=1, source_target_pairs={{1,5},{3,7},{5,1},{7,3},{9,13},{11,15},{13,9},{15,11},{17,21},{19,... | collective-permute-start | bytes 12296 | tf_op jit(solution)/shard_map/ppermute | solution.py:368
  25.7 0.7 %collective-permute-start.5 = (f32[8,128]{1,0:T(8,128)S(1)}, f32[8,128]{1,0:T(8,128)S(1)}, u32[]{:S(2)}, u32[]{:S(2)}) collective-permute-start(f32[8,128]{1,0:T(8,128)S(1)} %max.17), channel_id=1, source_target_pairs={{1,9},{3,11},{5,13},{7,15},{9,1},{11,3},{13,5},{15,7},{17,25},{19,... | collective-permute-start | bytes 12296 | tf_op jit(solution)/shard_map/ppermute | solution.py:368
  26.4 14.0 %collective-permute-start.6 = (f32[8,128]{1,0:T(8,128)S(1)}, f32[8,128]{1,0:T(8,128)S(1)}, u32[]{:S(2)}, u32[]{:S(2)}) collective-permute-start(f32[8,128]{1,0:T(8,128)S(1)} %max.18), channel_id=1, source_target_pairs={{1,0},{3,2},{5,4},{7,6},{9,8},{11,10},{13,12},{15,14},{17,16},{19,... | collective-permute-start | bytes 12296 | tf_op jit(solution)/shard_map/ppermute | solution.py:370
where the time goes:
time: 40.6 us; the launch traced here: 40.9 us
  waiting for transfers between devices  14.8 us (36%)
  Pallas kernels  13.1 us (32%)
  starting transfers between devices  10.5 us (26%)
  between operations  2.04 us (5%)
  local copies, waits for them, and re-layouts  0.52 us (1%)
    ppermute x1, waiting for transfers between devices, largest(): lax.ppermute(value, axis, [(i, i - 1) for i in odd])  11.6 us
    pallas_call x1, Pallas kernels, body(): pl.pallas_call(spread_kernel, out_shape=(layer_pair, layer_pair, pltpu.VM...  6.12 us
    ppermute x1, starting transfers between devices, body(): far_new = lax.ppermute(far, 'gx', far_pairs)  6 us
    pallas_call x1, Pallas kernels, body(): pl.pallas_call(collect_kernel, out_shape=(jax.ShapeDtypeStruct((blocks, 8...  5.92 us
    ppermute x1, waiting for transfers between devices, body(): far_new = lax.ppermute(far, 'gx', far_pairs)  1.99 us
    ppermute x3, starting transfers between devices, largest(): value = jnp.maximum(value, lax.ppermute(value, axis, pairs))  1.97 us
    ppermute x1, starting transfers between devices, largest(): lax.ppermute(value, axis, [(i, i - 1) for i in odd])  1.29 us
    ppermute x1, waiting for transfers between devices, largest(): lax.ppermute(value, axis, [(i, i ^ 1) for i in range(devices)])  1.15 us
  transfers between devices with their start and end apart: 7, of which 3 were waited for; matrix products, arithmetic and copies ran while one was open for 0% of the time, Pallas kernels for 2%

commit v1 on v0

--- a/solution.py
+++ b/solution.py
@@ -357,17 +357,17 @@
 
 def largest(value, axis):
     devices = lax.axis_size(axis)
-    value = jnp.maximum(value, lax.ppermute(value, axis, [(i, i ^ 1) for i in range(devices)]))
-    odd = range(1, devices, 2)
+    swap = [(i, i ^ 1) for i in range(devices)]
+    value = jnp.maximum(value, lax.ppermute(value, axis, swap))
     reach = 2
     while reach < devices:
         if devices & (devices - 1) == 0:
-            pairs = [(i, i ^ reach) for i in odd]
+            pairs = [(i, i ^ reach if i % 2 else i) for i in range(devices)]
         else:
-            pairs = [(i, (i + reach) % devices) for i in odd]
+            pairs = [(i, (i + reach) % devices if i % 2 else i) for i in range(devices)]
         value = jnp.maximum(value, lax.ppermute(value, axis, pairs))
         reach *= 2
-    return jnp.maximum(value, lax.ppermute(value, axis, [(i, i - 1) for i in odd]))
+    return jnp.maximum(value, lax.ppermute(value, axis, swap))
 
 
 smem = pl.BlockSpec(memory_space=pltpu.SMEM)

time: 40.6 us -> 39.8 us (0.980); the launches traced: 40.9 us -> 39.7 us
  waiting for transfers between devices: 14.8 us -> 3.15 us
  starting transfers between devices: 10.5 us -> 21.6 us
  Pallas kernels: 13.1 us -> 12.4 us
    ppermute x2, waiting for transfers between devices: 12.8 us -> 1.16 us  [the longest x1 1.15 us: largest(): value = jnp.maximum(value, lax.ppermute(value, axis, swap))]
    ppermute x2, starting transfers between devices: 1.36 us -> 12.1 us  [the longest x1 12.1 us: largest(): return jnp.maximum(value, lax.ppermute(value, axis, swap))]
    ppermute x1, starting transfers between devices: 6 us -> 6.63 us  [body(): far_new = lax.ppermute(far, 'gx', far_pairs)]
  transfers between devices with their start and end apart: 7 -> 7, of which waited for: 3 -> 2; matrix products, arithmetic and copies ran while one was open for 0% -> 0% of each run, Pallas kernels for 2% -> 3%
where the time goes in v1:
time: 39.8 us; the launch traced here: 39.7 us
  starting transfers between devices  21.6 us (54%)
  Pallas kernels  12.4 us (31%)
  waiting for transfers between devices  3.15 us (8%)
  between operations  2.04 us (5%)
  local copies, waits for them, and re-layouts  0.52 us (1%)
    ppermute x1, starting transfers between devices, largest(): return jnp.maximum(value, lax.ppermute(value, axis, swap))  12.1 us
    ppermute x1, starting transfers between devices, body(): far_new = lax.ppermute(far, 'gx', far_pairs)  6.63 us
    pallas_call x1, Pallas kernels, body(): pl.pallas_call(spread_kernel, out_shape=(layer_pair, layer_pair, pltpu.VM...  5.79 us
    pallas_call x1, Pallas kernels, body(): pl.pallas_call(collect_kernel, out_shape=(jax.ShapeDtypeStruct((blocks, 8...  5.58 us
    ppermute x1, waiting for transfers between devices, body(): far_new = lax.ppermute(far, 'gx', far_pairs)  1.99 us
    ppermute x3, starting transfers between devices, largest(): value = jnp.maximum(value, lax.ppermute(value, axis, pairs))  1.97 us
    ppermute x1, waiting for transfers between devices, largest(): value = jnp.maximum(value, lax.ppermute(value, axis, swap))  1.15 us
    pallas_call x1, Pallas kernels, body(): pl.pallas_call(finish_kernel, out_shape=(jax.ShapeDtypeStruct(frac.shape,...  1 us
  transfers between devices with their start and end apart: 7, of which 2 were waited for; matrix products, arithmetic and copies ran while one was open for 0% of the time, Pallas kernels for 3%

profile of v1, /device:TPU:0, one launch (start us, length us, event | category | flops | bytes accessed | tf_op | source)
XLA Modules:
  0.0 39.7 jit_solution(13109903241267647847)
XLA Ops:
  1.3 5.8 %spread.1 = (f32[8,32,128]{2,1,0:T(8,128)S(1)}, f32[8,32,128]{2,1,0:T(8,128)S(1)}, s32[8,128]{1,0:T(8,128)S(1)}, f32[3,16384]{1,0:T(4,128)S(1)}, f32[3,16384]{1,0:T(4,128)S(1)}, /*index=5*/s32[128,128]{1,0:T(8,128)S(1)}) custom-call(s32[1]{0:T(128)S(6)} %copy.9.count_ref, f32[3,16384]{1,0:T(4,128)} %frac_hbm.1, f32[3,16384]{1,0:T(4,128)} %vel_hbm.1, ...), custom_call_target="tpu_custom_call" | custom-call | tf_op jit(solution)/shard_map/spread/pallas_call | solution.py:384
  7.1 0.8 %collective-permute-start.1 = (f32[8,32,128]{2,1,0:T(8,128)S(1)}, f32[8,32,128]{2,1,0:T(8,128)S(1)}, u32[]{:S(2)}, u32[]{:S(2)}) collective-permute-start(f32[8,32,128]{2,1,0:T(8,128)S(1)} %get-tuple-element.14.near_ref), channel_id=1, source_target_pairs={{0,1},{1,0},{2,3},{3,2},{4,5},{5,4},{6,7},{7,6},{8,9},{9,8},{10,11... | collective-permute-start | bytes 393224 | tf_op jit(solution)/shard_map/ppermute | solution.py:409
  7.9 6.6 %collective-permute-start = (f32[8,32,128]{2,1,0:T(8,128)S(1)}, f32[8,32,128]{2,1,0:T(8,128)S(1)}, u32[]{:S(2)}, u32[]{:S(2)}) collective-permute-start(f32[8,32,128]{2,1,0:T(8,128)S(1)} %get-tuple-element.15.far_ref), channel_id=1, source_target_pairs={{0,15},{1,2},{2,1},{3,4},{4,3},{5,6},{6,5},{7,8},{8,7},{9,10},{10,... | collective-permute-start | bytes 393224 | tf_op jit(solution)/shard_map/ppermute | solution.py:410
  15.2 0.0 collective-permute-done.1.near_new_ref
  15.2 2.0 %collective-permute-done.far_new_ref = f32[8,32,128]{2,1,0:T(8,128)S(1)} collective-permute-done((f32[8,32,128]{2,1,0:T(8,128)S(1)}, f32[8,32,128]{2,1,0:T(8,128)S(1)}, u32[]{:S(2)}, u32[]{:S(2)}) %collective-permute-start) | collective-permute-done | bytes 131104 | tf_op jit(solution)/shard_map/ppermute | solution.py:410
  17.2 5.6 %collect.1 = (f32[64,8,256]{2,1,0:T(8,128)S(1)}, f32[8,128]{1,0:T(8,128)S(1)}) custom-call(f32[1]{0:T(128)S(6)} %copy.10.step_ref, s32[8,128]{1,0:T(8,128)S(1)} %get-tuple-element.13.plan_ref, f32[8,32,128]{2,1,0:T(8,128)S(1)} %get-tuple-element.14.near_ref, f32[8,32,128]{2,1,0:T(8,128)S(1)} %get-tuple-element.15.far_ref, ...), custom_call_target="tpu_custom_call" | custom-call | tf_op jit(solution)/shard_map/collect/pallas_call | solution.py:411
  22.8 0.1 collective-permute-start.2
  22.8 1.2 %collective-permute-done.2 = f32[8,128]{1,0:T(8,128)S(1)} collective-permute-done((f32[8,128]{1,0:T(8,128)S(1)}, f32[8,128]{1,0:T(8,128)S(1)}, u32[]{:S(2)}, u32[]{:S(2)}) %collective-permute-start.2) | collective-permute-done | bytes 4128 | tf_op jit(solution)/shard_map/ppermute | solution.py:361
  24.0 0.7 %collective-permute-start.3 = (f32[8,128]{1,0:T(8,128)S(1)}, f32[8,128]{1,0:T(8,128)S(1)}, u32[]{:S(2)}, u32[]{:S(2)}) collective-permute-start(f32[8,128]{1,0:T(8,128)S(1)} %max.15), channel_id=1, source_target_pairs={{0,0},{1,3},{2,2},{3,1},{4,4},{5,7},{6,6},{7,5},{8,8},{9,11},{10,1... | collective-permute-start | bytes 12296 | tf_op jit(solution)/shard_map/ppermute | solution.py:368
  24.7 0.0 collective-permute-done.3
  24.7 0.7 %collective-permute-start.4 = (f32[8,128]{1,0:T(8,128)S(1)}, f32[8,128]{1,0:T(8,128)S(1)}, u32[]{:S(2)}, u32[]{:S(2)}) collective-permute-start(f32[8,128]{1,0:T(8,128)S(1)} %max.16), channel_id=1, source_target_pairs={{0,0},{1,5},{2,2},{3,7},{4,4},{5,1},{6,6},{7,3},{8,8},{9,13},{10,1... | collective-permute-start | bytes 12296 | tf_op jit(solution)/shard_map/ppermute | solution.py:368
  25.4 0.0 collective-permute-done.4
  25.4 0.7 %collective-permute-start.5 = (f32[8,128]{1,0:T(8,128)S(1)}, f32[8,128]{1,0:T(8,128)S(1)}, u32[]{:S(2)}, u32[]{:S(2)}) collective-permute-start(f32[8,128]{1,0:T(8,128)S(1)} %max.17), channel_id=1, source_target_pairs={{0,0},{1,9},{2,2},{3,11},{4,4},{5,13},{6,6},{7,15},{8,8},{9,1},{10... | collective-permute-start | bytes 12296 | tf_op jit(solution)/shard_map/ppermute | solution.py:368
  26.0 0.0 collective-permute-done.5
  26.1 12.1 %collective-permute-start.6 = (f32[8,128]{1,0:T(8,128)S(1)}, f32[8,128]{1,0:T(8,128)S(1)}, u32[]{:S(2)}, u32[]{:S(2)}) collective-permute-start(f32[8,128]{1,0:T(8,128)S(1)} %max.18), channel_id=1, source_target_pairs={{0,1},{1,0},{2,3},{3,2},{4,5},{5,4},{6,7},{7,6},{8,9},{9,8},{10,11... | collective-permute-start | bytes 12296 | tf_op jit(solution)/shard_map/ppermute | solution.py:370
  38.1 1.0 %finish.1 = (f32[3,16384]{1,0:T(4,128)}, f32[3,16384]{1,0:T(4,128)}) custom-call(s32[8,128]{1,0:T(8,128)S(1)} %get-tuple-element.13.plan_ref, f32[64,8,256]{2,1,0:T(8,128)S(1)} %get-tuple-element.19.moved_ref, f32[3,16384]{1,0:T(4,128)S(1)} %get-tuple-element.16.frac_ref), custom_call_target="tpu_custom_call" | custom-call | bytes 8000000 | tf_op jit(solution)/shard_map/finish/pallas_call | solution.py:428
  39.1 0.0 collective-permute-done.6
  39.2 0.5 %slice.3 = f32[1,1]{1,0:T(1,128)} slice(f32[8,128]{1,0:T(8,128)S(1)} %add_divide_fusion), slice={[0:1], [0:1]} | slice | bytes 8 | tf_op jit(solution)/shard_map/slice | solution.py:441
  (5 shorter events, 0.0 us)
Async XLA Ops:
  7.1 8.1 %collective-permute-start.1 = (f32[8,32,128]{2,1,0:T(8,128)S(1)}, f32[8,32,128]{2,1,0:T(8,128)S(1)}, u32[]{:S(2)}, u32[]{:S(2)}) collective-permute-start(f32[8,32,128]{2,1,0:T(8,128)S(1)} %get-tuple-element.14.near_ref), channel_id=1, source_target_pairs={{0,1},{1,0},{2,3},{3,2},{4,5},{5,4},{6,7},{7,6},{8,9},{9,8},{10,11... | collective-permute-start | bytes 393224 | tf_op jit(solution)/shard_map/ppermute | solution.py:409
  7.9 9.3 %collective-permute-start = (f32[8,32,128]{2,1,0:T(8,128)S(1)}, f32[8,32,128]{2,1,0:T(8,128)S(1)}, u32[]{:S(2)}, u32[]{:S(2)}) collective-permute-start(f32[8,32,128]{2,1,0:T(8,128)S(1)} %get-tuple-element.15.far_ref), channel_id=1, source_target_pairs={{0,15},{1,2},{2,1},{3,4},{4,3},{5,6},{6,5},{7,8},{8,7},{9,10},{10,... | collective-permute-start | bytes 393224 | tf_op jit(solution)/shard_map/ppermute | solution.py:410
  22.8 1.2 %collective-permute-start.2 = (f32[8,128]{1,0:T(8,128)S(1)}, f32[8,128]{1,0:T(8,128)S(1)}, u32[]{:S(2)}, u32[]{:S(2)}) collective-permute-start(f32[8,128]{1,0:T(8,128)S(1)} %get-tuple-element.22), channel_id=1, source_target_pairs={{0,1},{1,0},{2,3},{3,2},{4,5},{5,4},{6,7},{7,6},{8,9},{9,8},{10,11... | collective-permute-start | bytes 12296 | tf_op jit(solution)/shard_map/ppermute | solution.py:361
  24.0 0.7 %collective-permute-start.3 = (f32[8,128]{1,0:T(8,128)S(1)}, f32[8,128]{1,0:T(8,128)S(1)}, u32[]{:S(2)}, u32[]{:S(2)}) collective-permute-start(f32[8,128]{1,0:T(8,128)S(1)} %max.15), channel_id=1, source_target_pairs={{0,0},{1,3},{2,2},{3,1},{4,4},{5,7},{6,6},{7,5},{8,8},{9,11},{10,1... | collective-permute-start | bytes 12296 | tf_op jit(solution)/shard_map/ppermute | solution.py:368
  24.7 0.7 %collective-permute-start.4 = (f32[8,128]{1,0:T(8,128)S(1)}, f32[8,128]{1,0:T(8,128)S(1)}, u32[]{:S(2)}, u32[]{:S(2)}) collective-permute-start(f32[8,128]{1,0:T(8,128)S(1)} %max.16), channel_id=1, source_target_pairs={{0,0},{1,5},{2,2},{3,7},{4,4},{5,1},{6,6},{7,3},{8,8},{9,13},{10,1... | collective-permute-start | bytes 12296 | tf_op jit(solution)/shard_map/ppermute | solution.py:368
  25.4 0.7 %collective-permute-start.5 = (f32[8,128]{1,0:T(8,128)S(1)}, f32[8,128]{1,0:T(8,128)S(1)}, u32[]{:S(2)}, u32[]{:S(2)}) collective-permute-start(f32[8,128]{1,0:T(8,128)S(1)} %max.17), channel_id=1, source_target_pairs={{0,0},{1,9},{2,2},{3,11},{4,4},{5,13},{6,6},{7,15},{8,8},{9,1},{10... | collective-permute-start | bytes 12296 | tf_op jit(solution)/shard_map/ppermute | solution.py:368
  26.1 13.1 %collective-permute-start.6 = (f32[8,128]{1,0:T(8,128)S(1)}, f32[8,128]{1,0:T(8,128)S(1)}, u32[]{:S(2)}, u32[]{:S(2)}) collective-permute-start(f32[8,128]{1,0:T(8,128)S(1)} %max.18), channel_id=1, source_target_pairs={{0,1},{1,0},{2,3},{3,2},{4,5},{5,4},{6,7},{7,6},{8,9},{9,8},{10,11... | collective-permute-start | bytes 12296 | tf_op jit(solution)/shard_map/ppermute | solution.py:370
